TPU v7x, 32 devices: a whole 2x2x4 slice. The times are simulated.
32 devices in a mesh: groups: 2 (over y), tm: 4 (over x, core), space: 4 (over z).
Axes of the slice: x: 2, y: 2, z: 4, core: 2. Of those that a mesh axis runs over, the one named last changes fastest.
Arguments:
- initial_state: float32 [8, 32, 8, 128], P(None, ('groups', 'space')), parts along dimension 1, may hold values from -3 to 3
- first_guess: float32 [32, 8, 32, 8, 128], P('tm', None, ('groups', 'space')), parts along dimension 2, may hold values from -3 to 3
- diffusivity: float32 [8, 32, 8, 128], P(None, ('groups', 'space')), parts along dimension 1, may hold values from 0.02 to 0.2
- growth_rates: float32 [8], replicated, may hold values from -1 to 1
- coupling: float32 [8, 8], replicated, may hold values from -2 to 2
Outputs:
- iterate: float32 [32, 8, 32, 8, 128], P('tm', None, ('groups', 'space')), parts along dimension 2
There are 2 independent parts, one for each index of `groups`. A program takes and returns all parts, laid end to end along the dimension named above; an argument that names none is the same for every part. Nothing has to cross between parts.
All inputs are finite; a program needn't handle non-finite values.
Results may differ from a plain program's by a relative error of at most 0.0001.
Values sent between devices are 32-bit elements; how exact they have to be, the bound alone decides.
A program may use at most 64 MiB of HBM per device.

v0:
```python
import jax
import jax.numpy as jnp
from jax import lax
from jax.sharding import PartitionSpec as P

SWEEPS = 2


slab_span = 0.025


def extended(block, sides, width):
    for axis, dim in sides:
        count = lax.axis_size(axis)
        forward = [(i, i + 1) for i in range(count - 1)]
        backward = [(target, source) for source, target in forward]
        low = lax.ppermute(
            lax.slice_in_dim(block, block.shape[dim] - width, None, axis=dim), axis, forward
        )
        high = lax.ppermute(lax.slice_in_dim(block, 0, width, axis=dim), axis, backward)
        block = jnp.concatenate([low, block, high], axis=dim)
    return block


def evaluate(coeffs, point):
    result = 0.0
    for entry in reversed(coeffs):
        result = result * point + entry
    return result


def quadrature(node_count):
    node_pos = [(index + 0.5) / node_count for index in range(node_count)]
    within_rows = [[0.0] * node_count for row_no in range(node_count)]
    whole_row = [0.0] * node_count
    for column in range(node_count):
        coeffs = [1.0]
        scale_value = 1.0
        for other_node in range(node_count):
            if other_node != column:
                shifted = [0.0] + coeffs
                for degree in range(len(coeffs)):
                    shifted[degree] = shifted[degree] - node_pos[other_node] * coeffs[degree]
                coeffs = shifted
                scale_value = scale_value * (node_pos[column] - node_pos[other_node])
        antider = [0.0] + [
            coeffs[degree] / (degree + 1) / scale_value for degree in range(len(coeffs))
        ]
        for row_no in range(node_count):
            within_rows[row_no][column] = evaluate(antider, node_pos[row_no]) * slab_span
        whole_row[column] = evaluate(antider, 1.0) * slab_span
    return (within_rows, whole_row)


def fourth(field, axis_no):
    return (
        16.0 * (jnp.roll(field, 1, axis_no) + jnp.roll(field, -1, axis_no))
        - (jnp.roll(field, 2, axis_no) + jnp.roll(field, -2, axis_no))
        - 30.0 * field
    ) / 12.0


def tendency(padded, center, diffusivity, growth_rates, coupling):
    along_x = (
        16.0 * (padded[:, :, 3:-1] + padded[:, :, 1:-3])
        - (padded[:, :, 4:] + padded[:, :, :-4])
        - 30.0 * center
    ) / 12.0
    laplace = along_x + fourth(center, 3) + fourth(center, 4)
    mixing = jnp.einsum("sr,nrxyz->nsxyz", coupling, center, precision=lax.Precision.HIGHEST)
    return (
        diffusivity[None] * laplace
        + growth_rates[None, :, None, None, None] * center
        - center * center * center / 3.0
        + mixing
    )


def on_device(initial_state, first_guess, diffusivity, growth_rates, coupling):
    node_count = first_guess.shape[0]
    within_rows, whole_row = quadrature(node_count)
    within_table = jnp.asarray(within_rows, jnp.float32)
    whole_table = jnp.asarray(whole_row, jnp.float32)
    my_slab = lax.axis_index("tm")
    iterate = first_guess
    for sweep_no in range(SWEEPS):
        padded = extended(iterate, (("space", 2),), 2)
        forcing = tendency(padded, iterate, diffusivity, growth_rates, coupling)
        local_part = jnp.einsum(
            "mj,jsxyz->msxyz", within_table, forcing, precision=lax.Precision.HIGHEST
        )
        slab_total = jnp.einsum(
            "j,jsxyz->sxyz", whole_table, forcing, precision=lax.Precision.HIGHEST
        )
        shard_rows = lax.all_gather(slab_total[None], "tm", axis=0, tiled=True)
        slab_ids = jnp.arange(shard_rows.shape[0], dtype=jnp.int32)
        earlier = (slab_ids < my_slab).astype(jnp.float32)
        preceding = jnp.sum(earlier[:, None, None, None, None] * shard_rows, axis=0)
        iterate = initial_state[None] + preceding[None] + local_part
    return iterate


def solution(mesh):
    in_specs = (
        P(None, ("groups", "space"), None, None),
        P("tm", None, ("groups", "space"), None, None),
        P(None, ("groups", "space"), None, None),
        P(),
        P(),
    )
    out_specs = P("tm", None, ("groups", "space"), None, None)
    return jax.shard_map(
        on_device, mesh=mesh, in_specs=in_specs, out_specs=out_specs, check_vma=False
    )
```

profile of v0, /device:TPU:11, one launch (start us, length us, event | category | flops | bytes accessed | tf_op | source)
XLA Modules:
  0.0 84.6 jit_solution(6052795613059193162)
XLA Ops:
  0.0 1.3 %fusion.63 = (f32[8,8,2,8,128]{4,3,2,1,0:T(8,128)S(1)}, f32[8,8,2,8,128]{4,3,2,1,0:T(8,128)S(1)}) fusion(f32[8,8,4,8,128]{4,3,2,1,0:T(8,128)} %param.8), kind=kLoop, calls=%fused_computation.95 | loop fusion | bytes 2097152 | tf_op jit(solution)/shard_map/slice | solution.py:20
  1.3 1.0 %copy.93 = f32[8,8,2,8,128]{4,1,3,2,0:T(8,128)} copy(f32[8,8,2,8,128]{4,3,2,1,0:T(8,128)S(1)} %get-tuple-element.40) | data formatting | bytes 1048576
  2.3 3.2 %collective-permute-start.1 = (f32[8,8,2,8,128]{4,1,3,2,0:T(8,128)}, f32[8,8,2,8,128]{4,1,3,2,0:T(8,128)}, u32[]{:S(2)}, u32[]{:S(2)}) collective-permute-start(f32[8,8,2,8,128]{4,1,3,2,0:T(8,128)} %copy.93), channel_id=1, source_target_pairs={{0,1},{1,2},{2,3},{4,5},{5,6},{6,7},{8,9},{9,10},{10,11},{12,13},{... | collective-permute-start | bytes 1572872 | tf_op jit(solution)/shard_map/ppermute | solution.py:17
  5.5 1.0 %copy.94 = f32[8,8,2,8,128]{4,1,3,2,0:T(8,128)} copy(f32[8,8,2,8,128]{4,3,2,1,0:T(8,128)S(1)} %get-tuple-element.39) | data formatting | bytes 1048576
  6.5 2.9 %collective-permute-start = (f32[8,8,2,8,128]{4,1,3,2,0:T(8,128)}, f32[8,8,2,8,128]{4,1,3,2,0:T(8,128)}, u32[]{:S(2)}, u32[]{:S(2)}) collective-permute-start(f32[8,8,2,8,128]{4,1,3,2,0:T(8,128)} %copy.94), channel_id=1, source_target_pairs={{1,0},{2,1},{3,2},{5,4},{6,5},{7,6},{9,8},{10,9},{11,10},{13,12},{... | collective-permute-start | bytes 1572872 | tf_op jit(solution)/shard_map/ppermute | solution.py:20
  9.4 0.4 fusion.57
  9.8 0.4 fusion.58
  10.1 0.4 fusion.55
  10.5 0.4 fusion.56
  10.9 0.3 fusion.61
  11.1 0.3 fusion.59
  11.6 0.6 copy.103
  12.2 0.6 copy.104
  12.8 1.6 %copy.105 = f32[8,8,4,8,1]{4,1,3,2,0:T(8,128)} copy(f32[8,8,4,8,1]{4,3,2,1,0:T(8,128)S(1)} %get-tuple-element.29) | data formatting | bytes 16384
  14.4 1.6 %copy.106 = f32[8,8,4,8,127]{4,1,3,2,0:T(8,128)} copy(f32[8,8,4,8,127]{4,3,2,1,0:T(8,128)S(1)} %get-tuple-element.27) | data formatting | bytes 2080768
  16.0 1.6 %copy.107 = f32[8,8,4,8,126]{4,1,3,2,0:T(8,128)} copy(f32[8,8,4,8,126]{4,3,2,1,0:T(8,128)S(1)} %get-tuple-element.24) | data formatting | bytes 2064384
  17.6 1.6 %copy.108 = f32[8,8,4,8,2]{4,1,3,2,0:T(8,128)} copy(f32[8,8,4,8,2]{4,3,2,1,0:T(8,128)S(1)} %get-tuple-element.26) | data formatting | bytes 32768
  19.2 1.6 %copy.109 = f32[8,8,4,8,2]{4,1,3,2,0:T(8,128)} copy(f32[8,8,4,8,2]{4,3,2,1,0:T(8,128)S(1)} %get-tuple-element.25) | data formatting | bytes 32768
  20.8 1.6 %copy.110 = f32[8,8,4,8,126]{4,1,3,2,0:T(8,128)} copy(f32[8,8,4,8,126]{4,3,2,1,0:T(8,128)S(1)} %get-tuple-element.23) | data formatting | bytes 2064384
  22.3 1.5 %copy.95 = f32[8,8,4,7,128]{4,1,3,2,0:T(8,128)} copy(f32[8,8,4,7,128]{4,3,2,1,0:T(8,128)S(1)} %get-tuple-element.36) | data formatting | bytes 1835008
  23.8 1.5 %copy.98 = f32[8,8,4,7,128]{4,1,3,2,0:T(8,128)} copy(f32[8,8,4,7,128]{4,3,2,1,0:T(8,128)S(1)} %get-tuple-element.35) | data formatting | bytes 1835008
  25.3 1.4 %copy.102 = f32[8,8,4,6,128]{4,1,3,2,0:T(8,128)} copy(f32[8,8,4,6,128]{4,3,2,1,0:T(8,128)S(1)} %get-tuple-element.31) | data formatting | bytes 1572864
  26.7 1.4 %copy.99 = f32[8,8,4,6,128]{4,1,3,2,0:T(8,128)} copy(f32[8,8,4,6,128]{4,3,2,1,0:T(8,128)S(1)} %get-tuple-element.32) | data formatting | bytes 1572864
  28.1 0.8 copy.101
  29.0 0.7 copy.96
  29.7 0.7 copy.97
  30.5 1.2 %constant_dynamic-update-slice_fusion.3 = f32[8,8,6,8,128]{4,1,3,2,0:T(8,128)S(1)} fusion(f32[8,8,2,8,128]{4,1,3,2,0:T(8,128)} %collective-permute-done.1), kind=kLoop, calls=%fused_computation.73 | loop fusion | bytes 1048576
  31.7 0.6 constant_dynamic-update-slice_fusion.1
  32.3 1.4 %constant_dynamic-update-slice_fusion = f32[8,8,6,8,128]{4,1,3,2,0:T(8,128)S(1)} fusion(f32[8,8,6,8,128]{4,1,3,2,0:T(8,128)S(1)} %get-tuple-element.41, f32[8,8,2,8,128]{4,1,3,2,0:T(8,128)} %collective-permute-done), kind=kLoop, calls=%fused_computation.70 | loop fusion | bytes 1048576 | tf_op jit(solution)/shard_map/concatenate | solution.py:21
  33.8 0.2 copy-done.5
  34.0 5.2 %fusion.2 = f32[8,8,4,8,128]{4,1,3,2,0:T(8,128)S(1)} fusion(f32[8,8,6,8,128]{4,1,3,2,0:T(8,128)S(1)} %get-tuple-element.42, f32[8,8,6,8,128]{4,1,3,2,0:T(8,128)S(1)} %constant_dynamic-update-slice_fusion, f32[8,8,4,7,128]{4,1,3,2,0:T(8,128)} %copy.95, f32[8,8,4,1,128]{4,1,3,2,0:T(8,128)} %copy.96, f32[8,8,4,1,128]{4,1,3,2,0:T(8,128)} %copy.97, ...), kind=kOutput, calls=%fused_computation.11 | convolution fusion | flops 34078720 | bytes 20042240 | tf_op jit(solution)/shard_map/sr,nrxyz->nsxyz/dot_general | solution.py:70
  39.3 1.6 %fusion.39 = f32[1,8,4,8,128]{4,0,3,2,1:T(1,128)S(1)} fusion(f32[8,1,1,1,1]{0,1,4,3,2:T(1,128)S(1)} %copy-done.10, f32[8,8,4,8,128]{4,1,3,2,0:T(8,128)S(1)} %fusion.2), kind=kOutput, calls=%fused_computation.63 | convolution fusion | flops 3145728 | bytes 1179680 | tf_op jit(solution)/shard_map/j,jsxyz->sxyz/dot_general | solution.py:92
  40.9 7.6 %all-gather = f32[32,4,8,128]{3,2,1,0:T(8,128)S(1)} all-gather(f32[8,4,8,128]{3,2,1,0:T(8,128)S(1)} %bitcast.41), channel_id=2, replica_groups=mesh['groups'=2,'tm'=4,'space'=4] {'tm'}, dimensions={0}, use_global_device_ids=true | all-gather | bytes 655360 | tf_op jit(solution)/shard_map/all_gather | solution.py:95
  48.7 1.6 %fusion.41 = f32[8,4,8,128,8]{3,4,2,1,0:T(8,128)S(1)} fusion(f32[8,8,1,1,1]{1,0,4,3,2:T(8,128)S(1)} %copy-done.9, f32[8,8,4,8,128]{4,1,3,2,0:T(8,128)S(1)} %fusion.2), kind=kOutput, calls=%fused_computation.65 | convolution fusion | flops 25165824 | bytes 2097408 | tf_op jit(solution)/shard_map/mj,jsxyz->msxyz/dot_general | solution.py:89
  50.3 0.6 fusion.35
  50.9 0.4 fusion.48
  51.3 0.4 fusion.49
  51.7 0.4 fusion.46
  52.5 1.9 %collective-permute-start.2 = (f32[8,8,2,8,128]{4,1,3,2,0:T(8,128)S(1)}, f32[8,8,2,8,128]{4,1,3,2,0:T(8,128)S(1)}, u32[]{:S(2)}, u32[]{:S(2)}) collective-permute-start(f32[8,8,2,8,128]{4,1,3,2,0:T(8,128)S(1)} %get-tuple-element.21), channel_id=1, source_target_pairs={{1,0},{2,1},{3,2},{5,4},{6,5},{7,6},{9,8},{10,9},{11,10},{13,12},{... | collective-permute-start | bytes 1572872 | tf_op jit(solution)/shard_map/ppermute | solution.py:20
  54.4 3.4 %collective-permute-start.3 = (f32[8,8,2,8,128]{4,1,3,2,0:T(8,128)S(1)}, f32[8,8,2,8,128]{4,1,3,2,0:T(8,128)S(1)}, u32[]{:S(2)}, u32[]{:S(2)}) collective-permute-start(f32[8,8,2,8,128]{4,1,3,2,0:T(8,128)S(1)} %get-tuple-element.22), channel_id=1, source_target_pairs={{0,1},{1,2},{2,3},{4,5},{5,6},{6,7},{8,9},{9,10},{10,11},{12,13},{... | collective-permute-start | bytes 1572872 | tf_op jit(solution)/shard_map/ppermute | solution.py:17
  57.8 0.4 fusion.47
  58.2 9.6 %collective-permute-done.2 = f32[8,8,2,8,128]{4,1,3,2,0:T(8,128)S(1)} collective-permute-done((f32[8,8,2,8,128]{4,1,3,2,0:T(8,128)S(1)}, f32[8,8,2,8,128]{4,1,3,2,0:T(8,128)S(1)}, u32[]{:S(2)}, u32[]{:S(2)}) %collective-permute-start.2) | collective-permute-done | bytes 524320 | tf_op jit(solution)/shard_map/ppermute | solution.py:20
  67.8 1.9 %collective-permute-done.3 = f32[8,8,2,8,128]{4,1,3,2,0:T(8,128)S(1)} collective-permute-done((f32[8,8,2,8,128]{4,1,3,2,0:T(8,128)S(1)}, f32[8,8,2,8,128]{4,1,3,2,0:T(8,128)S(1)}, u32[]{:S(2)}, u32[]{:S(2)}) %collective-permute-start.3) | collective-permute-done | bytes 524320 | tf_op jit(solution)/shard_map/ppermute | solution.py:17
  69.7 2.7 %fusion.1 = f32[8,8,4,8,128]{4,1,3,2,0:T(8,128)S(1)} fusion(f32[8,8,4,8,128]{4,1,3,2,0:T(8,128)S(1)} %fusion.35, f32[8,8,2,8,128]{4,1,3,2,0:T(8,128)S(1)} %collective-permute-done.3, f32[8,8,2,8,128]{4,1,3,2,0:T(8,128)S(1)} %collective-permute-done.2, f32[8,8,4,7,128]{4,1,3,2,0:T(8,128)S(1)} %get-tuple-element.18, ...), kind=kOutput, calls=%fused_computation.9 | convolution fusion | flops 35127296 | bytes 16912896 | tf_op jit(solution)/shard_map/sr,nrxyz->nsxyz/dot_general | solution.py:70
  72.4 1.6 %fusion.36 = f32[1,8,4,8,128]{4,0,3,2,1:T(1,128)S(1)} fusion(f32[8,1,1,1,1]{0,1,4,3,2:T(1,128)S(1)} %copy-done.10, f32[8,8,4,8,128]{4,1,3,2,0:T(8,128)S(1)} %fusion.1), kind=kOutput, calls=%fused_computation.60 | convolution fusion | flops 3145728 | bytes 1179680 | tf_op jit(solution)/shard_map/j,jsxyz->sxyz/dot_general | solution.py:92
  74.0 7.7 %all-gather.1 = f32[32,4,8,128]{3,2,1,0:T(8,128)S(1)} all-gather(f32[8,4,8,128]{3,2,1,0:T(8,128)S(1)} %bitcast.40), channel_id=3, replica_groups=mesh['groups'=2,'tm'=4,'space'=4] {'tm'}, dimensions={0}, use_global_device_ids=true | all-gather | bytes 655360 | tf_op jit(solution)/shard_map/all_gather | solution.py:95
  81.8 1.6 %fusion = f32[8,8,4,8,128]{4,0,3,2,1:T(8,128)S(1)} fusion(f32[8,8,1,1,1]{1,0,4,3,2:T(8,128)S(1)} %copy-done.9, f32[8,8,4,8,128]{4,1,3,2,0:T(8,128)S(1)} %fusion.1, f32[8,4,8,128]{3,2,1,0:T(8,128)S(1)} %add.114), kind=kOutput, calls=%fused_computation.7 | convolution fusion | flops 25427968 | bytes 2228480 | tf_op jit(solution)/shard_map/mj,jsxyz->msxyz/dot_general | solution.py:89
  83.4 1.2 %copy.71 = f32[8,8,4,8,128]{4,3,2,1,0:T(8,128)} copy(f32[8,8,4,8,128]{4,0,3,2,1:T(8,128)S(1)} %fusion) | data formatting | bytes 2097152 | tf_op jit(solution)/shard_map/add | solution.py:99
  (41 shorter events, 1.4 us)
Async XLA Ops:
  0.0 33.8 %copy-start = (f32[8,8]{1,0:T(8,128)S(1)}, f32[8,8]{1,0:T(8,128)}, u32[]{:S(2)}) copy-start(f32[8,8]{1,0:T(8,128)} %param.11) | copy-start | bytes 772
  1.3 8.0 %copy-start.1 = (f32[8,8,4,8,128]{4,3,2,1,0:T(8,128)S(1)}, f32[8,8,4,8,128]{4,3,2,1,0:T(8,128)}, u32[]{:S(2)}) copy-start(f32[8,8,4,8,128]{4,3,2,1,0:T(8,128)} %param.8) | copy-start | bytes 3145732
  2.3 28.1 %collective-permute-start.1 = (f32[8,8,2,8,128]{4,1,3,2,0:T(8,128)}, f32[8,8,2,8,128]{4,1,3,2,0:T(8,128)}, u32[]{:S(2)}, u32[]{:S(2)}) collective-permute-start(f32[8,8,2,8,128]{4,1,3,2,0:T(8,128)} %copy.93), channel_id=1, source_target_pairs={{0,1},{1,2},{2,3},{4,5},{5,6},{6,7},{8,9},{9,10},{10,11},{12,13},{... | collective-permute-start | bytes 1572872 | tf_op jit(solution)/shard_map/ppermute | solution.py:17
  6.5 25.8 %collective-permute-start = (f32[8,8,2,8,128]{4,1,3,2,0:T(8,128)}, f32[8,8,2,8,128]{4,1,3,2,0:T(8,128)}, u32[]{:S(2)}, u32[]{:S(2)}) collective-permute-start(f32[8,8,2,8,128]{4,1,3,2,0:T(8,128)} %copy.94), channel_id=1, source_target_pairs={{1,0},{2,1},{3,2},{5,4},{6,5},{7,6},{9,8},{10,9},{11,10},{13,12},{... | collective-permute-start | bytes 1572872 | tf_op jit(solution)/shard_map/ppermute | solution.py:20
  26.7 3.7 %copy-start.8 = (f32[8,4,8,128]{3,2,1,0:T(8,128)S(1)}, f32[8,4,8,128]{3,2,1,0:T(8,128)}, u32[]{:S(2)}) copy-start(f32[8,4,8,128]{3,2,1,0:T(8,128)} %param.9) | copy-start | bytes 393220
  30.5 3.3 %copy-start.6 = (f32[8,8,4,8,2]{4,1,3,2,0:T(8,128)S(1)}, f32[8,8,4,8,2]{4,1,3,2,0:T(8,128)}, u32[]{:S(2)}) copy-start(f32[8,8,4,8,2]{4,1,3,2,0:T(8,128)} %copy.109) | copy-start | bytes 49156
  31.6 2.1 %copy-start.2 = (f32[8,8,4,8,1]{4,1,3,2,0:T(8,128)S(1)}, f32[8,8,4,8,1]{4,1,3,2,0:T(8,128)}, u32[]{:S(2)}) copy-start(f32[8,8,4,8,1]{4,1,3,2,0:T(8,128)} %copy.105) | copy-start | bytes 24580
  31.7 2.1 %copy-start.3 = (f32[8,8,4,8,127]{4,1,3,2,0:T(8,128)S(1)}, f32[8,8,4,8,127]{4,1,3,2,0:T(8,128)}, u32[]{:S(2)}) copy-start(f32[8,8,4,8,127]{4,1,3,2,0:T(8,128)} %copy.106) | copy-start | bytes 3121156
  31.7 2.1 %copy-start.4 = (f32[8,8,4,8,126]{4,1,3,2,0:T(8,128)S(1)}, f32[8,8,4,8,126]{4,1,3,2,0:T(8,128)}, u32[]{:S(2)}) copy-start(f32[8,8,4,8,126]{4,1,3,2,0:T(8,128)} %copy.107) | copy-start | bytes 3096580
  31.7 2.3 %copy-start.5 = (f32[8,8,4,8,2]{4,1,3,2,0:T(8,128)S(1)}, f32[8,8,4,8,2]{4,1,3,2,0:T(8,128)}, u32[]{:S(2)}) copy-start(f32[8,8,4,8,2]{4,1,3,2,0:T(8,128)} %copy.108) | copy-start | bytes 49156
  31.7 2.3 %copy-start.11 = (f32[8]{0:T(128)S(1)}, f32[8]{0:T(128)}, u32[]{:S(2)}) copy-start(f32[8]{0:T(128)} %param.10) | copy-start | bytes 100
  34.0 5.2 %copy-start.10 = (f32[8,1,1,1,1]{0,1,4,3,2:T(1,128)S(1)}, f32[8,1,1,1,1]{0,1,4,3,2:T(1,128)}, u32[]{:S(2)}) copy-start(f32[8,1,1,1,1]{0,1,4,3,2:T(1,128)} %constant.32) | copy-start | bytes 100
  39.2 9.3 %copy-start.7 = (f32[8,4,8,128]{3,2,1,0:T(8,128)S(1)}, f32[8,4,8,128]{3,2,1,0:T(8,128)}, u32[]{:S(2)}) copy-start(f32[8,4,8,128]{3,2,1,0:T(8,128)} %param.7) | copy-start | bytes 393220
  39.3 9.4 %copy-start.9 = (f32[8,8,1,1,1]{1,0,4,3,2:T(8,128)S(1)}, f32[8,8,1,1,1]{1,0,4,3,2:T(8,128)}, u32[]{:S(2)}) copy-start(f32[8,8,1,1,1]{1,0,4,3,2:T(8,128)} %constant.33) | copy-start | bytes 772
  52.5 15.3 %collective-permute-start.2 = (f32[8,8,2,8,128]{4,1,3,2,0:T(8,128)S(1)}, f32[8,8,2,8,128]{4,1,3,2,0:T(8,128)S(1)}, u32[]{:S(2)}, u32[]{:S(2)}) collective-permute-start(f32[8,8,2,8,128]{4,1,3,2,0:T(8,128)S(1)} %get-tuple-element.21), channel_id=1, source_target_pairs={{1,0},{2,1},{3,2},{5,4},{6,5},{7,6},{9,8},{10,9},{11,10},{13,12},{... | collective-permute-start | bytes 1572872 | tf_op jit(solution)/shard_map/ppermute | solution.py:20
  54.4 15.3 %collective-permute-start.3 = (f32[8,8,2,8,128]{4,1,3,2,0:T(8,128)S(1)}, f32[8,8,2,8,128]{4,1,3,2,0:T(8,128)S(1)}, u32[]{:S(2)}, u32[]{:S(2)}) collective-permute-start(f32[8,8,2,8,128]{4,1,3,2,0:T(8,128)S(1)} %get-tuple-element.22), channel_id=1, source_target_pairs={{0,1},{1,2},{2,3},{4,5},{5,6},{6,7},{8,9},{9,10},{10,11},{12,13},{... | collective-permute-start | bytes 1572872 | tf_op jit(solution)/shard_map/ppermute | solution.py:17
where the time goes:
time: 85.3 us; the launch traced here: 84.6 us
  local copies, waits for them, and re-layouts  30.8 us (36%)
  blocking collectives  15.3 us (18%)
  matrix products  14.3 us (17%)
  waiting for transfers between devices  11.5 us (13%)
  starting transfers between devices  11.3 us (13%)
  other arithmetic  0.9 us (1%)
    unnamed x44, local copies, waits for them, and re-layouts  22.5 us
    all_gather x2, blocking collectives, on_device(): shard_rows = lax.all_gather(slab_total[None], 'tm', axis=0, tiled=True)  15.3 us
    ppermute x2, waiting for transfers between devices, extended(): lax.ppermute(lax.slice_in_dim(block, 0, width, axis=dim), axis, backward)  9.57 us
    dot_general x2, matrix products, tendency(): jnp.einsum('sr,nrxyz->nsxyz', coupling, center, precision=lax.Precision.H...  7.9 us
    ppermute x2, starting transfers between devices, extended(): lax.ppermute(lax.slice_in_dim(block, block.shape[dim] - width, None, axis...  6.56 us
    ppermute x2, starting transfers between devices, extended(): lax.ppermute(lax.slice_in_dim(block, 0, width, axis=dim), axis, backward)  4.79 us
    dot_general x2, matrix products, on_device(): jnp.einsum('mj,jsxyz->msxyz', within_table, forcing, precision=lax.Precis...  3.19 us
    dot_general x2, matrix products, on_device(): jnp.einsum('j,jsxyz->sxyz', whole_table, forcing, precision=lax.Precision...  3.16 us
  transfers between devices with their start and end apart: 4, of which 2 were waited for; matrix products, arithmetic and copies ran while one was open for 28% of the time, Pallas kernels for 0%

commit v1 on v0

v1 whole, which is shorter than its diff:
```python
import functools

import jax
import jax.numpy as jnp
from jax import lax
from jax.experimental import pallas as pl
from jax.experimental.pallas import tpu as pltpu
from jax.sharding import PartitionSpec as P

MESH = pl.DeviceIdType.MESH
slab_span = 0.025


def evaluate(coeffs, point):
    result = 0.0
    for entry in reversed(coeffs):
        result = result * point + entry
    return result


def quadrature(node_count):
    node_pos = [(index + 0.5) / node_count for index in range(node_count)]
    within_rows = [[0.0] * node_count for row_no in range(node_count)]
    whole_row = [0.0] * node_count
    for column in range(node_count):
        coeffs = [1.0]
        scale_value = 1.0
        for other_node in range(node_count):
            if other_node != column:
                shifted = [0.0] + coeffs
                for degree in range(len(coeffs)):
                    shifted[degree] = shifted[degree] - node_pos[other_node] * coeffs[degree]
                coeffs = shifted
                scale_value = scale_value * (node_pos[column] - node_pos[other_node])
        antider = [0.0] + [
            coeffs[degree] / (degree + 1) / scale_value for degree in range(len(coeffs))
        ]
        for row_no in range(node_count):
            within_rows[row_no][column] = evaluate(antider, node_pos[row_no]) * slab_span
        whole_row[column] = evaluate(antider, 1.0) * slab_span
    return (within_rows, whole_row)


def kernel(
    n_tm, n_z, within, whole,
    guess, init, diff, coupling, growth, out,
    u, base, u1, hal, d12, tsend1, trecv1, tsend2, trecv2,
    load_sem, out_sem, hs1, hr1, hs2, hr2, ts1, tr1, ts2, tr2,
):
    nodes, species, planes = u.shape[:3]
    tm = lax.axis_index("tm")
    z = lax.axis_index("space")
    groups = ((1, 2), (0, planes - 1))

    can_send = (z < n_z - 1, z > 0)
    has_recv = (z > 0, z < n_z - 1)

    def target(side):
        return {"space": z + 1} if side == 0 else {"space": z - 1}

    def edge(side, dist):
        return planes - 1 - dist if side == 0 else dist

    def halo1(side, dist):
        return pltpu.make_async_remote_copy(
            src_ref=guess.at[:, :, edge(side, dist)],
            dst_ref=hal.at[0, side, dist],
            send_sem=hs1.at[side, dist], recv_sem=hr1.at[side, dist],
            device_id=target(side), device_id_type=MESH,
        )

    def halo2(side, dist, s):
        return pltpu.make_async_remote_copy(
            src_ref=u1.at[:, s, edge(side, dist)],
            dst_ref=hal.at[1, side, dist, :, s],
            send_sem=hs2.at[side, dist, s], recv_sem=hr2.at[side, dist, s],
            device_id=target(side), device_id_type=MESH,
        )

    def total1(source, peer, g):
        return pltpu.make_async_remote_copy(
            src_ref=tsend1.at[g], dst_ref=trecv1.at[source, g],
            send_sem=ts1.at[peer, g], recv_sem=tr1.at[source, g],
            device_id={"tm": peer}, device_id_type=MESH,
        )

    def total2(source, peer, s):
        return pltpu.make_async_remote_copy(
            src_ref=tsend2.at[s], dst_ref=trecv2.at[source, s],
            send_sem=ts2.at[peer, s], recv_sem=tr2.at[source, s],
            device_id={"tm": peer}, device_id_type=MESH,
        )

    def loop(count, body, first=0):
        def step(i, carry):
            body(i)
            return carry
        lax.fori_loop(first, count, step, 0)

    load = pltpu.make_async_copy(guess, u, load_sem)
    load.start()

    barrier = pltpu.get_barrier_semaphore()
    for side in (0, 1):
        @pl.when(can_send[side])
        def _():
            pl.semaphore_signal(barrier, inc=1, device_id=target(side), device_id_type=MESH)
    for peer in range(n_tm):
        @pl.when(peer != tm)
        def _():
            pl.semaphore_signal(barrier, inc=1, device_id={"tm": peer}, device_id_type=MESH)
    neighbours = (z > 0).astype(jnp.int32) + (z < n_z - 1).astype(jnp.int32)
    pl.semaphore_wait(barrier, neighbours + n_tm - 1)

    for dist in (0, 1):
        for side in (0, 1):
            @pl.when(can_send[side])
            def _():
                halo1(side, dist).start()

    for side in (0, 1):
        @pl.when(jnp.logical_not(has_recv[side]))
        def _():
            def clear(s):
                for k in (0, 1):
                    for dist in (0, 1):
                        hal[k, side, dist, :, s] = jnp.zeros(
                            (nodes,) + hal.shape[5:], jnp.float32)
            loop(species, clear)

    d12[...] = diff[...] * (1.0 / 12.0)
    load.wait()

    def near_part(ref, s, p):
        c = ref[:, s, p]
        acc = growth[s] * c - c * c * c * (1.0 / 3.0)
        for r in range(species):
            acc = acc + coupling[s, r] * ref[:, r, p]
        near = pltpu.roll(c, 1, 1) + pltpu.roll(c, c.shape[1] - 1, 1)
        near = near + (pltpu.roll(c, 1, 2) + pltpu.roll(c, c.shape[2] - 1, 2))
        far = pltpu.roll(c, 2, 1) + pltpu.roll(c, c.shape[1] - 2, 1)
        far = far + (pltpu.roll(c, 2, 2) + pltpu.roll(c, c.shape[2] - 2, 2))
        for q in (p - 1, p + 1):
            if 0 <= q < planes:
                near = near + ref[:, s, q]
        for q in (p - 2, p + 2):
            if 0 <= q < planes:
                far = far + ref[:, s, q]
        base[:, s, p] = acc + d12[s, p][None] * (16.0 * near - far - 90.0 * c)

    def with_halo(k, s, p):
        if p == 0:
            add = 16.0 * hal[k, 0, 0, :, s] - hal[k, 0, 1, :, s]
        elif p == 1:
            add = -hal[k, 0, 0, :, s]
        elif p == planes - 1:
            add = 16.0 * hal[k, 1, 0, :, s] - hal[k, 1, 1, :, s]
        else:
            add = -hal[k, 1, 0, :, s]
        return base[:, s, p] + d12[s, p][None] * add

    def integrate(f, s, p):
        for m in range(nodes):
            row = within[m][0] * f[0]
            for j in range(1, nodes):
                row = row + within[m][j] * f[j]
            base[m, s, p] = row
        total = whole[0] * f[0]
        for j in range(1, nodes):
            total = total + whole[j] * f[j]
        return total

    def all_near(ref):
        def body(s):
            for p in range(planes):
                near_part(ref, s, p)
        loop(species, body)

    all_near(u)
    for g in (0, 1):
        for side in (0, 1):
            @pl.when(has_recv[side])
            def _():
                halo1(side, g).wait_recv()

        def finish(s):
            for i, p in enumerate(groups[g]):
                tsend1[g, s, i] = integrate(with_halo(0, s, p), s, p)
        loop(species, finish)
        loop(n_tm, lambda peer: total1(tm, peer, g).start(), tm + 1)
        loop(tm, lambda source: total1(source, tm, g).wait_recv())

        def advance(s):
            for i, p in enumerate(groups[g]):
                first = lax.fori_loop(
                    0, tm, lambda q, acc: acc + trecv1[q, g, s, i],
                    jnp.zeros(init.shape[2:], jnp.float32))
                u1[:, s, p] = base[:, s, p] + (init[s, p] + first)[None]
            for side in (0, 1):
                @pl.when(can_send[side])
                def _():
                    halo2(side, 1 - g, s).start()
        loop(species, advance)

    all_near(u1)
    for side in (0, 1):
        @pl.when(has_recv[side])
        def _():
            loop(species, lambda s: halo2(side, 1, s).wait_recv())

    def finish2(s):
        for side in (0, 1):
            @pl.when(has_recv[side])
            def _():
                halo2(side, 0, s).wait_recv()
        for p in range(planes):
            tsend2[s, p] = integrate(with_halo(1, s, p), s, p)
        loop(n_tm, lambda peer: total2(tm, peer, s).start(), tm + 1)
    loop(species, finish2)

    def store(s):
        return pltpu.make_async_copy(u.at[:, s], out.at[:, s], out_sem.at[s])

    def last(s):
        def gather(q, acc):
            total2(q, tm, s).wait_recv()
            return acc + trecv2[q, s]
        first = lax.fori_loop(0, tm, gather, init[s])
        u[:, s] = base[:, s] + first[None]
        store(s).start()
    loop(species, last)

    for side in (0, 1):
        @pl.when(can_send[side])
        def _():
            for dist in (0, 1):
                halo1(side, dist).wait_send()
                loop(species, lambda s: halo2(side, dist, s).wait_send())

    def sent(peer):
        for g in (0, 1):
            total1(tm, peer, g).wait_send()
        loop(species, lambda s: total2(tm, peer, s).wait_send())
    loop(n_tm, sent, tm + 1)
    loop(species, lambda s: store(s).wait())


def on_device(n_tm, n_z, initial_state, first_guess, diffusivity, growth_rates, coupling):
    nodes, species, planes, cy, cz = first_guess.shape
    within, whole = quadrature(nodes)
    vmem = pl.BlockSpec(memory_space=pltpu.VMEM)
    smem = pl.BlockSpec(memory_space=pltpu.SMEM)
    anywhere = pl.BlockSpec(memory_space=pl.ANY)
    f32 = jnp.float32
    block = pltpu.VMEM(first_guess.shape, f32)
    dma = pltpu.SemaphoreType.DMA
    return pl.pallas_call(
        functools.partial(kernel, n_tm, n_z, within, whole),
        out_shape=jax.ShapeDtypeStruct(first_guess.shape, f32),
        in_specs=[anywhere, vmem, vmem, smem, smem],
        out_specs=anywhere,
        scratch_shapes=[
            block, block, block,
            pltpu.VMEM((2, 2, 2, nodes, species, cy, cz), f32),
            pltpu.VMEM((species, planes, cy, cz), f32),
            pltpu.VMEM((2, species, 2, cy, cz), f32),
            pltpu.VMEM((n_tm, 2, species, 2, cy, cz), f32),
            pltpu.VMEM((species, planes, cy, cz), f32),
            pltpu.VMEM((n_tm, species, planes, cy, cz), f32),
            dma, dma((species,)),
            dma((2, 2)), dma((2, 2)),
            dma((2, 2, species)), dma((2, 2, species)),
            dma((n_tm, 2)), dma((n_tm, 2)),
            dma((n_tm, species)), dma((n_tm, species)),
        ],
        compiler_params=pltpu.CompilerParams(
            collective_id=0, has_side_effects=True, vmem_limit_bytes=32 * 1024 * 1024
        ),
        cost_estimate=pl.CostEstimate(
            flops=2 * 60 * first_guess.size, bytes_accessed=9 * first_guess.size,
            transcendentals=0),
    )(first_guess, initial_state, diffusivity, coupling, growth_rates)


def solution(mesh):
    in_specs = (
        P(None, ("groups", "space"), None, None),
        P("tm", None, ("groups", "space"), None, None),
        P(None, ("groups", "space"), None, None),
        P(),
        P(),
    )
    out_specs = P("tm", None, ("groups", "space"), None, None)
    return jax.shard_map(
        functools.partial(on_device, mesh.shape["tm"], mesh.shape["space"]),
        mesh=mesh, in_specs=in_specs, out_specs=out_specs, check_vma=False,
    )
```

time: 85.3 us -> 37.5 us (0.44)
  Pallas kernels: 0 us -> 31.7 us
  local copies, waits for them, and re-layouts: 30.8 us -> 5.35 us
  blocking collectives: 15.3 us -> 0 us
  matrix products: 14.3 us -> 0 us
  waiting for transfers between devices: 11.5 us -> 0 us
  starting transfers between devices: 11.3 us -> 0 us
  other arithmetic: 0.9 us -> 0 us
    pallas_call x0 -> x1, Pallas kernels: none -> 31.7 us  [on_device(): pl.pallas_call(functools.partial(kernel, n_tm, n_z, within, whole), out_s...]
    unnamed x44 -> x11, local copies, waits for them, and re-layouts: 22.5 us -> 5.35 us
    all_gather x2 -> x0, blocking collectives: 15.3 us -> none  [on_device(): shard_rows = lax.all_gather(slab_total[None], 'tm', axis=0, tiled=True)]
    dot_general x6 -> x0, matrix products: 14.3 us -> none  [the longest x2 7.9 us: tendency(): jnp.einsum('sr,nrxyz->nsxyz', coupling, center, precision=lax.Precision.H...]
    ppermute x4 -> x0, waiting for transfers between devices: 11.5 us -> none  [the longest x2 9.57 us: extended(): lax.ppermute(lax.slice_in_dim(block, 0, width, axis=dim), axis, backward)]
    ppermute x4 -> x0, starting transfers between devices: 11.3 us -> none  [the longest x2 6.56 us: extended(): lax.ppermute(lax.slice_in_dim(block, block.shape[dim] - width, None, axis...]
    slice x18 -> x0, local copies, waits for them, and re-layouts: 5.58 us -> none  [the longest x8 2.12 us: fourth(): jnp.roll(field, -2, axis_no)]
    concatenate x1 -> x0, local copies, waits for them, and re-layouts: 1.41 us -> none  [extended(): block = jnp.concatenate([low, block, high], axis=dim)]
  transfers between devices with their start and end apart: 4 -> 0, of which waited for: 2 -> 0; matrix products, arithmetic and copies ran while one was open for 28% -> 0% of each run, Pallas kernels for 0% -> 0%
where the time goes in v1:
time: 37.5 us; the launch traced here: 37 us
  Pallas kernels  31.7 us (85%)
  local copies, waits for them, and re-layouts  5.35 us (14%)
    pallas_call x1, Pallas kernels, on_device(): pl.pallas_call(functools.partial(kernel, n_tm, n_z, within, whole), out_s...  31.7 us
    unnamed x11, local copies, waits for them, and re-layouts  5.35 us

profile of v1, /device:TPU:11, one launch (start us, length us, event | category | flops | bytes accessed | tf_op | source)
XLA Modules:
  0.0 37.0 jit_solution(7399250970873037356)
XLA Ops:
  0.0 0.0 copy-start
  0.0 1.2 %copy-done = f32[8,8,4,8,128]{4,3,2,1,0:T(8,128)S(1)} copy-done((f32[8,8,4,8,128]{4,3,2,1,0:T(8,128)S(1)}, f32[8,8,4,8,128]{4,3,2,1,0:T(8,128)}, u32[]{:S(2)}) %copy-start) | copy-done | bytes 1048600
  1.2 0.0 copy-start.1
  1.2 0.9 %copy-done.1 = f32[8,4,8,128]{3,2,1,0:T(8,128)S(1)} copy-done((f32[8,4,8,128]{3,2,1,0:T(8,128)S(1)}, f32[8,4,8,128]{3,2,1,0:T(8,128)}, u32[]{:S(2)}) %copy-start.1) | copy-done | bytes 131096
  2.1 0.0 copy-start.2
  2.1 0.9 %copy-done.2 = f32[8,4,8,128]{3,2,1,0:T(8,128)S(1)} copy-done((f32[8,4,8,128]{3,2,1,0:T(8,128)S(1)}, f32[8,4,8,128]{3,2,1,0:T(8,128)}, u32[]{:S(2)}) %copy-start.2) | copy-done | bytes 131096
  3.0 0.0 copy-start.3
  3.0 0.7 %copy-done.3 = f32[8,8]{1,0:T(8,128)S(1)} copy-done((f32[8,8]{1,0:T(8,128)S(1)}, f32[8,8]{1,0:T(8,128)}, u32[]{:S(2)}) %copy-start.3) | copy-done | bytes 280
  3.7 0.0 copy-start.4
  3.7 0.7 %copy-done.4 = f32[8]{0:T(128)S(1)} copy-done((f32[8]{0:T(128)S(1)}, f32[8]{0:T(128)}, u32[]{:S(2)}) %copy-start.4) | copy-done | bytes 56
  4.4 31.7 %shard_map.55 = f32[8,8,4,8,128]{4,3,2,1,0:T(8,128)S(1)} custom-call(f32[8,8,4,8,128]{4,3,2,1,0:T(8,128)S(1)} %copy-done, f32[8,4,8,128]{3,2,1,0:T(8,128)S(1)} %copy-done.1, f32[8,4,8,128]{3,2,1,0:T(8,128)S(1)} %copy-done.2, f32[8,8]{1,0:T(8,128)S(1)} %copy-done.3, f32[8]{0:T(128)S(1)} %copy-done.4), custom_call_target="tpu_custom_call" | custom-call | flops 31457280 | bytes 2359296 | tf_op jit(solution)/shard_map/pallas_call | solution.py:257
  36.0 1.0 %copy.7 = f32[8,8,4,8,128]{4,3,2,1,0:T(8,128)} copy(f32[8,8,4,8,128]{4,3,2,1,0:T(8,128)S(1)} %shard_map.55) | data formatting | bytes 2097152
Async XLA Ops:
  0.0 1.2 %copy-start = (f32[8,8,4,8,128]{4,3,2,1,0:T(8,128)S(1)}, f32[8,8,4,8,128]{4,3,2,1,0:T(8,128)}, u32[]{:S(2)}) copy-start(f32[8,8,4,8,128]{4,3,2,1,0:T(8,128)} %guess.1) | copy-start | bytes 3145732
  1.2 0.9 %copy-start.1 = (f32[8,4,8,128]{3,2,1,0:T(8,128)S(1)}, f32[8,4,8,128]{3,2,1,0:T(8,128)}, u32[]{:S(2)}) copy-start(f32[8,4,8,128]{3,2,1,0:T(8,128)} %init.1) | copy-start | bytes 393220
  2.1 0.9 %copy-start.2 = (f32[8,4,8,128]{3,2,1,0:T(8,128)S(1)}, f32[8,4,8,128]{3,2,1,0:T(8,128)}, u32[]{:S(2)}) copy-start(f32[8,4,8,128]{3,2,1,0:T(8,128)} %diff.1) | copy-start | bytes 393220
  3.0 0.7 %copy-start.3 = (f32[8,8]{1,0:T(8,128)S(1)}, f32[8,8]{1,0:T(8,128)}, u32[]{:S(2)}) copy-start(f32[8,8]{1,0:T(8,128)} %coupling.1) | copy-start | bytes 772
  3.7 0.7 %copy-start.4 = (f32[8]{0:T(128)S(1)}, f32[8]{0:T(128)}, u32[]{:S(2)}) copy-start(f32[8]{0:T(128)} %growth.1) | copy-start | bytes 100

commit v2 on v1

--- a/solution.py
+++ b/solution.py
@@ -43,7 +43,8 @@
 
 def kernel(
     n_tm, n_z, within, whole,
-    guess, init, diff, coupling, growth, out,
+    guess, init_in, diff_in, coupling_in, growth_in, out,
+    init, diff, coupling, growth, small_sem,
     u, base, u1, hal, d12, tsend1, trecv1, tsend2, trecv2,
     load_sem, out_sem, hs1, hr1, hs2, hr2, ts1, tr1, ts2, tr2,
 ):
@@ -99,6 +100,13 @@
 
     load = pltpu.make_async_copy(guess, u, load_sem)
     load.start()
+    small = [
+        pltpu.make_async_copy(source, target_ref, small_sem.at[i])
+        for i, (source, target_ref) in enumerate(
+            ((init_in, init), (diff_in, diff), (coupling_in, coupling), (growth_in, growth)))
+    ]
+    for copy in small:
+        copy.start()
 
     barrier = pltpu.get_barrier_semaphore()
     for side in (0, 1):
@@ -112,11 +120,10 @@
     neighbours = (z > 0).astype(jnp.int32) + (z < n_z - 1).astype(jnp.int32)
     pl.semaphore_wait(barrier, neighbours + n_tm - 1)
 
-    for dist in (0, 1):
-        for side in (0, 1):
-            @pl.when(can_send[side])
-            def _():
-                halo1(side, dist).start()
+    for side in (0, 1):
+        @pl.when(can_send[side])
+        def _():
+            halo1(side, 0).start()
 
     for side in (0, 1):
         @pl.when(jnp.logical_not(has_recv[side]))
@@ -128,6 +135,8 @@
                             (nodes,) + hal.shape[5:], jnp.float32)
             loop(species, clear)
 
+    for copy in small:
+        copy.wait()
     d12[...] = diff[...] * (1.0 / 12.0)
     load.wait()
 
@@ -177,6 +186,11 @@
         loop(species, body)
 
     all_near(u)
+    for side in (0, 1):
+        @pl.when(can_send[side])
+        def _():
+            halo1(side, 0).wait_send()
+            halo1(side, 1).start()
     for g in (0, 1):
         for side in (0, 1):
             @pl.when(has_recv[side])
@@ -233,8 +247,8 @@
     for side in (0, 1):
         @pl.when(can_send[side])
         def _():
+            halo1(side, 1).wait_send()
             for dist in (0, 1):
-                halo1(side, dist).wait_send()
                 loop(species, lambda s: halo2(side, dist, s).wait_send())
 
     def sent(peer):
@@ -248,18 +262,21 @@
 def on_device(n_tm, n_z, initial_state, first_guess, diffusivity, growth_rates, coupling):
     nodes, species, planes, cy, cz = first_guess.shape
     within, whole = quadrature(nodes)
-    vmem = pl.BlockSpec(memory_space=pltpu.VMEM)
-    smem = pl.BlockSpec(memory_space=pltpu.SMEM)
-    anywhere = pl.BlockSpec(memory_space=pl.ANY)
+    hbm = pl.BlockSpec(memory_space=pltpu.HBM)
     f32 = jnp.float32
     block = pltpu.VMEM(first_guess.shape, f32)
     dma = pltpu.SemaphoreType.DMA
     return pl.pallas_call(
         functools.partial(kernel, n_tm, n_z, within, whole),
         out_shape=jax.ShapeDtypeStruct(first_guess.shape, f32),
-        in_specs=[anywhere, vmem, vmem, smem, smem],
-        out_specs=anywhere,
+        in_specs=[hbm] * 5,
+        out_specs=hbm,
         scratch_shapes=[
+            pltpu.VMEM((species, planes, cy, cz), f32),
+            pltpu.VMEM((species, planes, cy, cz), f32),
+            pltpu.SMEM(coupling.shape, f32),
+            pltpu.SMEM(growth_rates.shape, f32),
+            dma((4,)),
             block, block, block,
             pltpu.VMEM((2, 2, 2, nodes, species, cy, cz), f32),
             pltpu.VMEM((species, planes, cy, cz), f32),
@@ -274,7 +291,7 @@
             dma((n_tm, species)), dma((n_tm, species)),
         ],
         compiler_params=pltpu.CompilerParams(
-            collective_id=0, has_side_effects=True, vmem_limit_bytes=32 * 1024 * 1024
+            collective_id=0, has_side_effects=True, vmem_limit_bytes=60 * 1024 * 1024
         ),
         cost_estimate=pl.CostEstimate(
             flops=2 * 60 * first_guess.size, bytes_accessed=9 * first_guess.size,

time: 37.5 us -> 34.8 us (0.928); the launches traced: 37 us -> 34.7 us
  local copies, waits for them, and re-layouts: 5.35 us -> 2.26 us
  Pallas kernels: 31.7 us -> 32.4 us
    unnamed x11 -> x1, local copies, waits for them, and re-layouts: 5.35 us -> 2.26 us
    pallas_call x1, Pallas kernels: 31.7 us -> 32.4 us  [on_device(): pl.pallas_call(functools.partial(kernel, n_tm, n_z, within, whole), out_s...]
where the time goes in v2:
time: 34.8 us; the launch traced here: 34.7 us
  Pallas kernels  32.4 us (93%)
  local copies, waits for them, and re-layouts  2.26 us (6%)
    pallas_call x1, Pallas kernels, on_device(): pl.pallas_call(functools.partial(kernel, n_tm, n_z, within, whole), out_s...  32.4 us
    unnamed x1, local copies, waits for them, and re-layouts  2.26 us

profile of v2, /device:TPU:11, one launch (start us, length us, event | category | flops | bytes accessed | tf_op | source)
XLA Modules:
  0.0 34.7 jit_solution(9336413524182223696)
XLA Ops:
  0.0 32.4 %shard_map.55 = f32[8,8,4,8,128]{4,3,2,1,0:T(8,128)} custom-call(f32[8,8,4,8,128]{4,3,2,1,0:T(8,128)} %guess.1, f32[8,4,8,128]{3,2,1,0:T(8,128)} %init_in.1, f32[8,4,8,128]{3,2,1,0:T(8,128)} %diff_in.1, f32[8,8]{1,0:T(8,128)} %coupling_in.1, f32[8]{0:T(128)} %growth_in.1), custom_call_target="tpu_custom_call" | custom-call | flops 31457280 | bytes 2359296 | tf_op jit(solution)/shard_map/pallas_call | solution.py:269
  32.4 2.3 %copy.7 = f32[8,8,4,8,128]{4,3,2,1,0:T(8,128)} copy(f32[8,8,4,8,128]{4,3,2,1,0:T(8,128)} %shard_map.55) | data formatting | bytes 2097152

commit v3 on v2

--- a/solution.py
+++ b/solution.py
@@ -270,7 +270,7 @@
         functools.partial(kernel, n_tm, n_z, within, whole),
         out_shape=jax.ShapeDtypeStruct(first_guess.shape, f32),
         in_specs=[hbm] * 5,
-        out_specs=hbm,
+        out_specs=pl.BlockSpec(memory_space=pl.ANY),
         scratch_shapes=[
             pltpu.VMEM((species, planes, cy, cz), f32),
             pltpu.VMEM((species, planes, cy, cz), f32),
@@ -291,7 +291,7 @@
             dma((n_tm, species)), dma((n_tm, species)),
         ],
         compiler_params=pltpu.CompilerParams(
-            collective_id=0, has_side_effects=True, vmem_limit_bytes=60 * 1024 * 1024
+            collective_id=0, has_side_effects=True, vmem_limit_bytes=32 * 1024 * 1024
         ),
         cost_estimate=pl.CostEstimate(
             flops=2 * 60 * first_guess.size, bytes_accessed=9 * first_guess.size,

time: 34.8 us -> 37.5 us (1.078)
  local copies, waits for them, and re-layouts: 2.26 us -> 5.35 us
  Pallas kernels: 32.4 us -> 32 us
    unnamed x1 -> x11, local copies, waits for them, and re-layouts: 2.26 us -> 5.35 us
    pallas_call x1, Pallas kernels: 32.4 us -> 32 us  [on_device(): pl.pallas_call(functools.partial(kernel, n_tm, n_z, within, whole), out_s...]
where the time goes in v3:
time: 37.5 us; the launch traced here: 37.3 us
  Pallas kernels  32 us (85%)
  local copies, waits for them, and re-layouts  5.35 us (14%)
    pallas_call x1, Pallas kernels, on_device(): pl.pallas_call(functools.partial(kernel, n_tm, n_z, within, whole), out_s...  32 us
    unnamed x11, local copies, waits for them, and re-layouts  5.35 us

profile of v3, /device:TPU:11, one launch (start us, length us, event | category | flops | bytes accessed | tf_op | source)
XLA Modules:
  0.0 37.3 jit_solution(10658049098916493347)
XLA Ops:
  0.0 0.0 copy-start
  0.0 1.2 %copy-done = f32[8,8,4,8,128]{4,3,2,1,0:T(8,128)S(1)} copy-done((f32[8,8,4,8,128]{4,3,2,1,0:T(8,128)S(1)}, f32[8,8,4,8,128]{4,3,2,1,0:T(8,128)}, u32[]{:S(2)}) %copy-start) | copy-done | bytes 1048600
  1.2 0.0 copy-start.1
  1.2 0.9 %copy-done.1 = f32[8,4,8,128]{3,2,1,0:T(8,128)S(1)} copy-done((f32[8,4,8,128]{3,2,1,0:T(8,128)S(1)}, f32[8,4,8,128]{3,2,1,0:T(8,128)}, u32[]{:S(2)}) %copy-start.1) | copy-done | bytes 131096
  2.1 0.0 copy-start.2
  2.1 0.9 %copy-done.2 = f32[8,4,8,128]{3,2,1,0:T(8,128)S(1)} copy-done((f32[8,4,8,128]{3,2,1,0:T(8,128)S(1)}, f32[8,4,8,128]{3,2,1,0:T(8,128)}, u32[]{:S(2)}) %copy-start.2) | copy-done | bytes 131096
  3.0 0.0 copy-start.3
  3.0 0.7 %copy-done.3 = f32[8,8]{1,0:T(8,128)S(1)} copy-done((f32[8,8]{1,0:T(8,128)S(1)}, f32[8,8]{1,0:T(8,128)}, u32[]{:S(2)}) %copy-start.3) | copy-done | bytes 280
  3.7 0.0 copy-start.4
  3.7 0.7 %copy-done.4 = f32[8]{0:T(128)S(1)} copy-done((f32[8]{0:T(128)S(1)}, f32[8]{0:T(128)}, u32[]{:S(2)}) %copy-start.4) | copy-done | bytes 56
  4.4 32.0 %shard_map.55 = f32[8,8,4,8,128]{4,3,2,1,0:T(8,128)S(1)} custom-call(f32[8,8,4,8,128]{4,3,2,1,0:T(8,128)S(1)} %copy-done, f32[8,4,8,128]{3,2,1,0:T(8,128)S(1)} %copy-done.1, f32[8,4,8,128]{3,2,1,0:T(8,128)S(1)} %copy-done.2, f32[8,8]{1,0:T(8,128)S(1)} %copy-done.3, f32[8]{0:T(128)S(1)} %copy-done.4), custom_call_target="tpu_custom_call" | custom-call | flops 31457280 | bytes 2359296 | tf_op jit(solution)/shard_map/pallas_call | solution.py:269
  36.3 1.0 %copy.7 = f32[8,8,4,8,128]{4,3,2,1,0:T(8,128)} copy(f32[8,8,4,8,128]{4,3,2,1,0:T(8,128)S(1)} %shard_map.55) | data formatting | bytes 2097152
Async XLA Ops:
  0.0 1.2 %copy-start = (f32[8,8,4,8,128]{4,3,2,1,0:T(8,128)S(1)}, f32[8,8,4,8,128]{4,3,2,1,0:T(8,128)}, u32[]{:S(2)}) copy-start(f32[8,8,4,8,128]{4,3,2,1,0:T(8,128)} %guess.1) | copy-start | bytes 3145732
  1.2 0.9 %copy-start.1 = (f32[8,4,8,128]{3,2,1,0:T(8,128)S(1)}, f32[8,4,8,128]{3,2,1,0:T(8,128)}, u32[]{:S(2)}) copy-start(f32[8,4,8,128]{3,2,1,0:T(8,128)} %init_in.1) | copy-start | bytes 393220
  2.1 0.9 %copy-start.2 = (f32[8,4,8,128]{3,2,1,0:T(8,128)S(1)}, f32[8,4,8,128]{3,2,1,0:T(8,128)}, u32[]{:S(2)}) copy-start(f32[8,4,8,128]{3,2,1,0:T(8,128)} %diff_in.1) | copy-start | bytes 393220
  3.0 0.7 %copy-start.3 = (f32[8,8]{1,0:T(8,128)S(1)}, f32[8,8]{1,0:T(8,128)}, u32[]{:S(2)}) copy-start(f32[8,8]{1,0:T(8,128)} %coupling_in.1) | copy-start | bytes 772
  3.7 0.7 %copy-start.4 = (f32[8]{0:T(128)S(1)}, f32[8]{0:T(128)}, u32[]{:S(2)}) copy-start(f32[8]{0:T(128)} %growth_in.1) | copy-start | bytes 100

commit v4 on v2

--- a/solution.py
+++ b/solution.py
@@ -124,6 +124,7 @@
         @pl.when(can_send[side])
         def _():
             halo1(side, 0).start()
+            halo1(side, 1).start()
 
     for side in (0, 1):
         @pl.when(jnp.logical_not(has_recv[side]))
@@ -190,7 +191,6 @@
         @pl.when(can_send[side])
         def _():
             halo1(side, 0).wait_send()
-            halo1(side, 1).start()
     for g in (0, 1):
         for side in (0, 1):
             @pl.when(has_recv[side])

time: 34.8 us -> 34 us (0.977)
  Pallas kernels: 32.4 us -> 31.5 us
    pallas_call x1, Pallas kernels: 32.4 us -> 31.5 us  [on_device(): pl.pallas_call(functools.partial(kernel, n_tm, n_z, within, whole), out_s...]
where the time goes in v4:
time: 34 us; the launch traced here: 33.8 us
  Pallas kernels  31.5 us (93%)
  local copies, waits for them, and re-layouts  2.26 us (7%)
    pallas_call x1, Pallas kernels, on_device(): pl.pallas_call(functools.partial(kernel, n_tm, n_z, within, whole), out_s...  31.5 us
    unnamed x1, local copies, waits for them, and re-layouts  2.26 us

profile of v4, /device:TPU:11, one launch (start us, length us, event | category | flops | bytes accessed | tf_op | source)
XLA Modules:
  0.0 33.8 jit_solution(14955598168254441421)
XLA Ops:
  0.0 31.5 %shard_map.55 = f32[8,8,4,8,128]{4,3,2,1,0:T(8,128)} custom-call(f32[8,8,4,8,128]{4,3,2,1,0:T(8,128)} %guess.1, f32[8,4,8,128]{3,2,1,0:T(8,128)} %init_in.1, f32[8,4,8,128]{3,2,1,0:T(8,128)} %diff_in.1, f32[8,8]{1,0:T(8,128)} %coupling_in.1, f32[8]{0:T(128)} %growth_in.1), custom_call_target="tpu_custom_call" | custom-call | flops 31457280 | bytes 2359296 | tf_op jit(solution)/shard_map/pallas_call | solution.py:269
  31.5 2.3 %copy.7 = f32[8,8,4,8,128]{4,3,2,1,0:T(8,128)} copy(f32[8,8,4,8,128]{4,3,2,1,0:T(8,128)} %shard_map.55) | data formatting | bytes 2097152
